TPU v7x, 32 devices: a whole 2x2x4 slice. The times are simulated.
32 devices in a mesh: groups: 2 (over y), sec: 4 (over z), term: 4 (over x, core).
Axes of the slice: x: 2, y: 2, z: 4, core: 2. Of those that a mesh axis runs over, the one named last changes fastest.
Arguments:
- wavefunction: bfloat16 [256, 3, 128, 128], P(('groups', 'sec')), parts along dimension 0, may hold values from -6 to 6
- left_ops: bfloat16 [256, 16, 128, 128], P(('groups', 'sec'), 'term'), parts along dimension 0, may hold values from -0.5 to 0.5
- right_ops: bfloat16 [256, 16, 128, 128], P(('groups', 'sec'), 'term'), parts along dimension 0, may hold values from -0.125 to 0.125
- sector_sizes: int32 [256], P('groups'), parts along dimension 0, may hold values from 16 to 128
- right_partner: int32 [256], P('groups'), parts along dimension 0, may hold values from 0 to 127, as said below
Outputs:
- sigma_blocks: float32 [256, 3, 128, 128], P(('groups', 'sec', 'term')), parts along dimension 0
There are 2 independent parts, one for each index of `groups`. A program takes and returns all parts, laid end to end along the dimension named above; each array names one. Nothing has to cross between parts.
Inputs may be any that keep to these rules, and one draw needn't show every extreme that they name: `right_partner`: a permutation of the 128 sectors; the 32 sectors of one device of sec have partners on at most 8 sectors of any one device, and this number is reached.
All inputs are finite; a program needn't handle non-finite values.
Results may differ from a plain program's by a relative error of at most 0.003.
Values may be sent and summed in bfloat16 or wider, within the bound.
A program may use at most 128 MiB of HBM per device.

v0:
```python
import jax
import jax.numpy as jnp
from jax import lax
from jax.sharding import PartitionSpec as P


def on_device(wavefunction, left_ops, right_ops, sector_sizes, right_partner):
    sector_count = wavefunction.shape[0]
    block_size = wavefunction.shape[2]
    peer_count = lax.axis_size("sec")
    own_index = lax.axis_index("sec")
    capacity = -(-sector_count // peer_count)
    slot_count = peer_count * capacity
    all_sectors = sector_sizes.shape[0]
    sector_ids = jnp.arange(all_sectors, dtype=jnp.int32)
    source_dev = sector_ids // sector_count
    target_dev = right_partner // sector_count
    earlier = (
        (source_dev[:, None] == source_dev[None, :])
        & (target_dev[:, None] == target_dev[None, :])
        & (sector_ids[None, :] < sector_ids[:, None])
    )
    rank_within = jnp.sum(earlier.astype(jnp.int32), axis=1)
    slot_of = target_dev * capacity + rank_within
    local_slot = lax.dynamic_slice_in_dim(slot_of, own_index * sector_count, sector_count)
    slot_range = jnp.arange(slot_count, dtype=jnp.int32)
    receive_key = jnp.where(target_dev == own_index, source_dev * capacity + rank_within, -1)
    receive_match = receive_key[None, :] == slot_range[:, None]
    receive_index = jnp.sum(
        jnp.where(receive_match, (right_partner % sector_count)[None, :], 0), axis=1
    )
    receive_valid = jnp.any(receive_match, axis=1)
    local_sizes = lax.dynamic_slice_in_dim(sector_sizes, own_index * sector_count, sector_count)
    local_partner = lax.dynamic_slice_in_dim(right_partner, own_index * sector_count, sector_count)
    right_sizes = jnp.sum(
        jnp.where(local_partner[:, None] == sector_ids[None, :], sector_sizes[None, :], 0), axis=1
    )
    row_ids = jnp.arange(block_size, dtype=jnp.int32)
    keep_mask = (row_ids[None, :] < local_sizes[:, None])[:, :, None] & (
        row_ids[None, :] < right_sizes[:, None]
    )[:, None, :]
    masked = jnp.where(keep_mask[:, None], wavefunction, jnp.zeros_like(wavefunction))
    partial_value = jnp.einsum(
        "stij,svjk->stvik", left_ops, masked, preferred_element_type=jnp.float32
    ).astype(jnp.bfloat16)
    picked = jnp.take(right_ops, receive_index, axis=0)
    outgoing = jnp.where(receive_valid[:, None, None, None], picked, jnp.zeros_like(picked))
    arrived = lax.all_to_all(outgoing, "sec", split_axis=0, concat_axis=0, tiled=True)
    paired = jnp.take(arrived, local_slot, axis=0)
    result = jnp.einsum(
        "stvik,stmk->svim", partial_value, paired, preferred_element_type=jnp.float32
    )
    result = jnp.where(keep_mask[:, None], result, jnp.zeros_like(result))
    return lax.psum_scatter(result, "term", scatter_dimension=0, tiled=True)


def solution(mesh):
    placed = (
        P(("groups", "sec"), None, None, None),
        P(("groups", "sec"), "term", None, None),
        P(("groups", "sec"), "term", None, None),
        P("groups"),
        P("groups"),
    )
    return jax.shard_map(
        on_device,
        mesh=mesh,
        in_specs=placed,
        out_specs=P(("groups", "sec", "term"), None, None, None),
        check_vma=False,
    )
```

profile of v0, /device:TPU:9, one launch (start us, length us, event | category | flops | bytes accessed | tf_op | source)
XLA Modules:
  0.0 197.0 jit_solution(14976881707485439572)
XLA Ops:
  6.5 0.7 and_select_fusion.2
  7.2 0.2 convert_reduce_fusion
  7.4 0.1 fusion.28
  7.5 0.1 select_reduce_fusion
  7.7 5.2 %gather_fusion = bf16[32,4,128,128]{3,2,1,0:T(8,128)(2,1)} fusion(bf16[32,4,128,128]{3,2,1,0:T(8,128)(2,1)} %param.9, s32[1024]{0:T(1024)S(1)} %pad_clamp_fusion.1), kind=kCustom, calls=%fused_computation.clone | custom fusion | bytes 8388736 | tf_op jit(solution)/shard_map/jit(_take)/gather | solution.py:46
  12.9 4.7 %select_select_fusion = bf16[32,4,128,128]{3,2,1,0:T(8,128)(2,1)} fusion(bf16[32,4,128,128]{3,2,1,0:T(8,128)(2,1)} %gather_fusion, pred[32]{0:T(512)(128)(4,1)S(1)} %compare_and_fusion.1, pred[32]{0:T(512)(128)(4,1)S(1)} %fusion.28), kind=kLoop, calls=%fused_computation.10 | loop fusion | flops 4194304 | bytes 8388672 | tf_op jit(solution)/shard_map/jit(_where)/select_n | solution.py:47
  17.6 0.0 copy-start
  17.6 0.0 copy-start.1
  17.6 5.0 %all-to-all-start = ((bf16[32,4,128,128]{3,2,1,0:T(8,128)(2,1)}), bf16[32,4,128,128]{3,2,1,0:T(8,128)(2,1)}, u32[]{:S(2)}, u32[]{:S(2)}) async-start(bf16[32,4,128,128]{3,2,1,0:T(8,128)(2,1)} %select_select_fusion), calls=%async_computation | async-start | bytes 8388608 | tf_op jit(solution)/shard_map/all_to_all | solution.py:48
  22.6 0.0 reduce-scatter.2.cloned.1.call-start
  22.7 0.0 copy-done
  22.7 0.1 dynamic_slice.10
  22.8 0.0 copy-done.1
  22.8 0.1 dynamic_slice.9
  22.8 0.1 compare_and_fusion
  22.9 0.2 select_reduce_fusion.1
  23.1 0.1 iota_compare_fusion.3
  23.2 0.7 broadcast_and_fusion
  23.9 88.0 %all-to-all-done = bf16[32,4,128,128]{3,2,1,0:T(8,128)(2,1)} async-done(((bf16[32,4,128,128]{3,2,1,0:T(8,128)(2,1)}), bf16[32,4,128,128]{3,2,1,0:T(8,128)(2,1)}, u32[]{:S(2)}, u32[]{:S(2)}) %all-to-all-start) | async-done | bytes 4194336 | tf_op jit(solution)/shard_map/all_to_all | solution.py:48
  112.0 5.3 %gather_fusion.1 = bf16[32,4,128,128]{3,2,1,0:T(8,128)(2,1)} fusion(bf16[32,4,128,128]{3,2,1,0:T(8,128)(2,1)} %all-to-all-done, s32[1024]{0:T(1024)S(1)} %pad_clamp_fusion), kind=kCustom, calls=%fused_computation.1.clone | custom fusion | bytes 8388736 | tf_op jit(solution)/shard_map/jit(_take)/gather | solution.py:49
  117.3 11.3 %bitcast_select_fusion = f32[32,3,128,128]{3,2,1,0:T(8,128)} fusion(pred[32,128,128]{2,1,0:T(8,128)(4,1)S(1)} %broadcast_and_fusion, bf16[32,4,128,128]{3,2,1,0:T(8,128)(2,1)} %gather_fusion.1, pred[32]{0:T(512)(128)(4,1)S(1)} %get-tuple-element.6, bf16[32,4,128,128]{3,2,1,0:T(8,128)(2,1)} %param.8, bf16[32,3,128,128]{3,2,1,0:T(8,128)(2,1)} %param.7), kind=kOutput, calls=%fused_computation.6 | convolution fusion | flops 3232759808 | bytes 18350112 | tf_op jit(solution)/shard_map/stvik,stmk->svim/dot_general | solution.py:50
  128.5 0.0 reduce-scatter.2.cloned.1.call-update
  128.6 61.6 %reduce-scatter.2.cloned.1.call-done = f32[8,3,128,128]{3,2,1,0:T(8,128)} async-done(((f32[32,3,128,128]{3,2,1,0:T(8,128)}), f32[8,3,128,128]{3,2,1,0:T(8,128)}) %reduce-scatter.2.cloned.1.call-update) | async-done | bytes 1572880 | tf_op jit(solution)/shard_map/reduce_scatter | solution.py:54
  (5 shorter events, 0.0 us)
Async XLA Ops:
  17.6 5.1 %copy-start = (s32[128]{0:T(128)S(1)}, s32[128]{0:T(128)}, u32[]{:S(2)}) copy-start(s32[128]{0:T(128)} %param.11) | copy-start | bytes 1540
  17.6 5.2 %copy-start.1 = (s32[128]{0:T(128)S(1)}, s32[128]{0:T(128)}, u32[]{:S(2)}) copy-start(s32[128]{0:T(128)} %param.10) | copy-start | bytes 1540
  17.6 94.4 %all-to-all-start = ((bf16[32,4,128,128]{3,2,1,0:T(8,128)(2,1)}), bf16[32,4,128,128]{3,2,1,0:T(8,128)(2,1)}, u32[]{:S(2)}, u32[]{:S(2)}) async-start(bf16[32,4,128,128]{3,2,1,0:T(8,128)(2,1)} %select_select_fusion), calls=%async_computation | async-start | bytes 8388608 | tf_op jit(solution)/shard_map/all_to_all | solution.py:48
  22.6 167.6 %reduce-scatter.2.cloned.1.call-start = ((), (), s32[]{:S(2)}) async-start(), calls=%async_computation.2 | async-start | bytes 7864320 | tf_op jit(solution)/shard_map/reduce_scatter | solution.py:54
Sparse Core Ops, SparseCore 0:
  128.7 61.4 reduce-scatter.1
where the time goes:
time: 199 us; the launch traced here: 197 us
  waiting for transfers between devices  150 us (75%)
  between operations  13.5 us (7%)
  matrix products  11.3 us (6%)
  local copies, waits for them, and re-layouts  10.7 us (5%)
  other arithmetic  6.84 us (3%)
  starting transfers between devices  5.06 us (3%)
    all_to_all x1, waiting for transfers between devices, on_device(): lax.all_to_all(outgoing, 'sec', split_axis=0, concat_axis=0, tiled=True)  88 us
    reduce_scatter x1, waiting for transfers between devices, on_device(): return lax.psum_scatter(result, 'term', scatter_dimension=0, tiled=True)  61.6 us
    dot_general x1, matrix products, on_device(): jnp.einsum('stvik,stmk->svim', partial_value, paired, preferred_element_t...  11.3 us
    gather x1, local copies, waits for them, and re-layouts, on_device(): paired = jnp.take(arrived, local_slot, axis=0)  5.31 us
    gather x1, local copies, waits for them, and re-layouts, on_device(): picked = jnp.take(right_ops, receive_index, axis=0)  5.24 us
    all_to_all x1, starting transfers between devices, on_device(): lax.all_to_all(outgoing, 'sec', split_axis=0, concat_axis=0, tiled=True)  5.02 us
    select_n x1, other arithmetic, on_device(): jnp.where(receive_valid[:, None, None, None], picked, jnp.zeros_like(pick...  4.69 us
  transfers between devices with their start and end apart: 2, of which 2 were waited for; matrix products, arithmetic and copies ran while one was open for 1% of the time, Pallas kernels for 0%

commit v1 on v0

v1 whole, which is shorter than its diff:
```python
import functools

import jax
import jax.numpy as jnp
from jax import lax
from jax.experimental import pallas as pl
from jax.experimental.pallas import tpu as pltpu
from jax.sharding import PartitionSpec as P

MESH = pl.DeviceIdType.MESH
CHUNKS = (32, 32, 32, 16, 16)
AHEAD = 2


def kernel(chunks, receive_index, slot_of, sizes, partner, wave_hbm, left_hbm, right_hbm, out_ref,
           wave, left, right, partial, *rest):
    n_chunks = len(chunks)
    outgoing, arrived, sums, landed = (rest[i * n_chunks:(i + 1) * n_chunks] for i in range(4))
    load_sem, send_sem, recv_sem, sum_send_sem, sum_recv_sem = rest[4 * n_chunks:]
    sector_count, vecs, block, _ = wave.shape
    terms = left.shape[1]
    peers = lax.axis_size("sec")
    owners = lax.axis_size("term")
    capacity = sector_count // peers
    owned = sector_count // owners
    me = lax.axis_index("sec")
    my_term = lax.axis_index("term")
    starts = [sum(chunks[:c]) for c in range(n_chunks)]

    right_load = pltpu.make_async_copy(right_hbm, right, load_sem.at[0])
    left_load = pltpu.make_async_copy(left_hbm, left, load_sem.at[1])
    wave_load = pltpu.make_async_copy(wave_hbm, wave, load_sem.at[2])
    right_load.start()
    left_load.start()
    wave_load.start()

    barrier = pltpu.get_barrier_semaphore()

    def greet_sec(i, carry):
        pl.semaphore_signal(barrier, inc=1, device_id={"sec": lax.rem(me + i, peers)}, device_id_type=MESH)
        return carry

    def greet_term(i, carry):
        pl.semaphore_signal(barrier, inc=1, device_id={"term": lax.rem(my_term + i, owners)}, device_id_type=MESH)
        return carry

    lax.fori_loop(1, peers, greet_sec, 0)
    lax.fori_loop(1, owners, greet_term, 0)
    right_load.wait()

    def pick(c, target, into, slot_base):
        def one(r, carry):
            index = receive_index[target * capacity + r]
            for t in range(terms):
                into[slot_base + r, :, t * block:(t + 1) * block] = right[index, t, starts[c]:starts[c] + chunks[c], :]
            return carry
        lax.fori_loop(0, capacity, one, 0)

    def block_copy(c, target):
        return pltpu.make_async_remote_copy(
            src_ref=outgoing[c].at[pl.ds(target * capacity, capacity)],
            dst_ref=arrived[c].at[pl.ds(me * capacity, capacity)],
            send_sem=send_sem.at[c, target],
            recv_sem=recv_sem.at[c, me],
            device_id={"sec": target},
            device_id_type=MESH,
        )

    def arrival(c, source):
        return pltpu.make_async_remote_copy(
            src_ref=outgoing[c].at[pl.ds(source * capacity, capacity)],
            dst_ref=arrived[c].at[pl.ds(source * capacity, capacity)],
            send_sem=send_sem.at[c, source],
            recv_sem=recv_sem.at[c, source],
            device_id={"sec": source},
            device_id_type=MESH,
        )

    def far_first(i):
        return lax.rem(me + 1 + lax.rem(i + peers // 2 - 1, peers - 1), peers)

    def launch(c):
        def one(i, carry):
            target = far_first(i)
            pick(c, target, outgoing[c], target * capacity)
            block_copy(c, target).start()
            return carry
        lax.fori_loop(0, peers - 1, one, 0)

    def sent(c):
        def one(i, carry):
            block_copy(c, far_first(i)).wait_send()
            return carry
        lax.fori_loop(0, peers - 1, one, 0)

    def arrive(c):
        def one(i, carry):
            arrival(c, far_first(i)).wait_recv()
            return carry
        lax.fori_loop(0, peers - 1, one, 0)

    def sum_copy(c, owner):
        return pltpu.make_async_remote_copy(
            src_ref=sums[c].at[owner],
            dst_ref=landed[c].at[my_term],
            send_sem=sum_send_sem.at[c, owner],
            recv_sem=sum_recv_sem.at[c, my_term],
            device_id={"term": owner},
            device_id_type=MESH,
        )

    def sum_arrival(c, source):
        return pltpu.make_async_remote_copy(
            src_ref=sums[c].at[source],
            dst_ref=landed[c].at[source],
            send_sem=sum_send_sem.at[c, source],
            recv_sem=sum_recv_sem.at[c, source],
            device_id={"term": source},
            device_id_type=MESH,
        )

    pl.semaphore_wait(barrier, peers - 1 + owners - 1)
    for c in range(min(AHEAD, n_chunks)):
        launch(c)
    for c in range(n_chunks):
        pick(c, me, arrived[c], me * capacity)

    left_load.wait()
    wave_load.wait()
    row_ids = lax.broadcasted_iota(jnp.int32, (block, block), 0)
    column_ids = lax.broadcasted_iota(jnp.int32, (block, block), 1)

    def first_products(l, carry):
        own_size = sizes[me * sector_count + l]
        right_size = sizes[partner[me * sector_count + l]]
        keep = (row_ids < own_size) & (column_ids < right_size)
        masked = jnp.concatenate(
            [jnp.where(keep, wave[l, v].astype(jnp.float32), 0.0).astype(jnp.bfloat16) for v in range(vecs)], axis=1
        )
        for t in range(terms):
            product = jnp.dot(left[l, t], masked, preferred_element_type=jnp.float32).astype(jnp.bfloat16)
            for v in range(vecs):
                partial[l, v * block:(v + 1) * block, t * block:(t + 1) * block] = product[:, v * block:(v + 1) * block]
        return carry

    lax.fori_loop(0, sector_count, first_products, 0)

    def second_product(c, l):
        return lax.dot_general(
            arrived[c][slot_of[l]], partial[l], (((1,), (1,)), ((), ())), preferred_element_type=jnp.float32
        )

    def finish(c):
        rows = pl.ds(starts[c], chunks[c])

        def wait_one(i, carry):
            sum_arrival(c, lax.rem(my_term + i, owners)).wait_recv()
            return carry
        lax.fori_loop(1, owners, wait_one, 0)

        def add(s, carry):
            total = out_ref[s, rows, :]
            for i in range(1, owners):
                total = total + landed[c][lax.rem(my_term + i, owners), s].astype(jnp.float32)
            out_ref[s, rows, :] = total
            return carry
        lax.fori_loop(0, owned, add, 0)

    for c in range(n_chunks):
        arrive(c)
        if c + AHEAD < n_chunks:
            launch(c + AHEAD)

        def for_owner(i, carry):
            owner = lax.rem(my_term + i, owners)

            def one(s, inner):
                sums[c][owner, s] = second_product(c, owner * owned + s).astype(jnp.bfloat16)
                return inner
            lax.fori_loop(0, owned, one, 0)
            sum_copy(c, owner).start()
            return carry
        lax.fori_loop(1, owners, for_owner, 0)

        def for_me(s, carry):
            out_ref[s, starts[c]:starts[c] + chunks[c], :] = second_product(c, my_term * owned + s)
            return carry
        lax.fori_loop(0, owned, for_me, 0)
        if c > 0:
            finish(c - 1)
    finish(n_chunks - 1)

    for c in range(n_chunks):
        sent(c)

        def sum_sent(i, carry):
            sum_copy(c, lax.rem(my_term + i, owners)).wait_send()
            return carry
        lax.fori_loop(1, owners, sum_sent, 0)


def on_device(wavefunction, left_ops, right_ops, sector_sizes, right_partner):
    sector_count, vecs, block = wavefunction.shape[:3]
    terms = left_ops.shape[1]
    peers = lax.axis_size("sec")
    owners = lax.axis_size("term")
    own_index = lax.axis_index("sec")
    term_index = lax.axis_index("term")
    capacity = sector_count // peers
    owned = sector_count // owners
    sector_ids = jnp.arange(sector_sizes.shape[0], dtype=jnp.int32)
    source_dev = sector_ids // sector_count
    target_dev = right_partner // sector_count
    earlier = (
        (source_dev[:, None] == source_dev[None, :])
        & (target_dev[:, None] == target_dev[None, :])
        & (sector_ids[None, :] < sector_ids[:, None])
    )
    rank_within = jnp.sum(earlier.astype(jnp.int32), axis=1)
    slot_of = target_dev * capacity + rank_within
    local_slot = lax.dynamic_slice_in_dim(slot_of, own_index * sector_count, sector_count)
    slot_range = jnp.arange(sector_count, dtype=jnp.int32)
    receive_key = jnp.where(target_dev == own_index, source_dev * capacity + rank_within, -1)
    receive_index = jnp.sum(
        jnp.where(receive_key[None, :] == slot_range[:, None], (right_partner % sector_count)[None, :], 0), axis=1
    )

    chunks = CHUNKS
    wide = terms * block
    columns = vecs * block
    n = len(chunks)
    vmem = lambda shape, dtype: pltpu.VMEM(shape, dtype)
    scratch = [
        vmem(wavefunction.shape, jnp.bfloat16),
        vmem(left_ops.shape, jnp.bfloat16),
        vmem(right_ops.shape, jnp.bfloat16),
        vmem((sector_count, columns, wide), jnp.bfloat16),
    ]
    scratch += [vmem((sector_count, rows, wide), jnp.bfloat16) for rows in chunks]
    scratch += [vmem((sector_count, rows, wide), jnp.bfloat16) for rows in chunks]
    scratch += [vmem((owners, owned, rows, columns), jnp.bfloat16) for rows in chunks]
    scratch += [vmem((owners, owned, rows, columns), jnp.bfloat16) for rows in chunks]
    scratch += [
        pltpu.SemaphoreType.DMA((3,)),
        pltpu.SemaphoreType.DMA((n, peers)),
        pltpu.SemaphoreType.DMA((n, peers)),
        pltpu.SemaphoreType.DMA((n, owners)),
        pltpu.SemaphoreType.DMA((n, owners)),
    ]
    smem = pl.BlockSpec(memory_space=pltpu.SMEM)
    anywhere = pl.BlockSpec(memory_space=pl.ANY)
    summed = pl.pallas_call(
        functools.partial(kernel, chunks),
        out_shape=jax.ShapeDtypeStruct((owned, block, columns), jnp.float32),
        in_specs=[smem, smem, smem, smem, anywhere, anywhere, anywhere],
        out_specs=pl.BlockSpec(memory_space=pltpu.VMEM),
        scratch_shapes=scratch,
        compiler_params=pltpu.CompilerParams(
            collective_id=0, has_side_effects=True, vmem_limit_bytes=52 * 1024 * 1024
        ),
        cost_estimate=pl.CostEstimate(
            flops=4 * sector_count * terms * vecs * block**3, bytes_accessed=16 * 1024 * 1024, transcendentals=0
        ),
    )(receive_index, local_slot, sector_sizes, right_partner, wavefunction, left_ops, right_ops)

    first = own_index * sector_count + term_index * owned
    own_sizes = lax.dynamic_slice_in_dim(sector_sizes, first, owned)
    own_partner = lax.dynamic_slice_in_dim(right_partner, first, owned)
    right_sizes = jnp.sum(jnp.where(own_partner[:, None] == sector_ids[None, :], sector_sizes[None, :], 0), axis=1)
    row_ids = jnp.arange(block, dtype=jnp.int32)
    keep = (row_ids[None, :] < own_sizes[:, None])[:, :, None] & (row_ids[None, :] < right_sizes[:, None])[:, None, :]
    sigma = summed.reshape(owned, block, vecs, block).transpose(0, 2, 3, 1)
    return jnp.where(keep[:, None], sigma, jnp.zeros_like(sigma))


def solution(mesh):
    placed = (
        P(("groups", "sec"), None, None, None),
        P(("groups", "sec"), "term", None, None),
        P(("groups", "sec"), "term", None, None),
        P("groups"),
        P("groups"),
    )
    return jax.shard_map(
        on_device,
        mesh=mesh,
        in_specs=placed,
        out_specs=P(("groups", "sec", "term"), None, None, None),
        check_vma=False,
    )
```

time: 199 us -> 120 us (0.60)
  waiting for transfers between devices: 150 us -> 0 us
  Pallas kernels: 0 us -> 113 us
  between operations: 13.5 us -> 0.04 us
  matrix products: 11.3 us -> 0 us
  local copies, waits for them, and re-layouts: 10.7 us -> 3.3 us
  starting transfers between devices: 5.06 us -> 0 us
  other arithmetic: 6.84 us -> 3.38 us
    pallas_call x0 -> x1, Pallas kernels: none -> 113 us  [on_device(): pl.pallas_call(functools.partial(kernel, chunks), out_shape=jax.ShapeDtyp...]
    all_to_all x1 -> x0, waiting for transfers between devices: 88 us -> none  [on_device(): lax.all_to_all(outgoing, 'sec', split_axis=0, concat_axis=0, tiled=True)]
    reduce_scatter x1 -> x0, waiting for transfers between devices: 61.6 us -> none  [on_device(): return lax.psum_scatter(result, 'term', scatter_dimension=0, tiled=True)]
    dot_general x1 -> x0, matrix products: 11.3 us -> none  [on_device(): jnp.einsum('stvik,stmk->svim', partial_value, paired, preferred_element_t...]
    gather x2 -> x0, local copies, waits for them, and re-layouts: 10.5 us -> none  [the longest x1 5.31 us: on_device(): paired = jnp.take(arrived, local_slot, axis=0)]
    all_to_all x1 -> x0, starting transfers between devices: 5.02 us -> none  [on_device(): lax.all_to_all(outgoing, 'sec', split_axis=0, concat_axis=0, tiled=True)]
    select_n x2 -> x1, other arithmetic: 4.69 us -> 1.3 us  [on_device(): return jnp.where(keep[:, None], sigma, jnp.zeros_like(sigma))]
  transfers between devices with their start and end apart: 2 -> 0, of which waited for: 2 -> 0; matrix products, arithmetic and copies ran while one was open for 1% -> 0% of each run, Pallas kernels for 0% -> 0%
where the time goes in v1:
time: 120 us
  Pallas kernels  113 us (94%)
  other arithmetic  3.38 us (3%)
  local copies, waits for them, and re-layouts  3.3 us (3%)
    pallas_call x1, Pallas kernels, on_device(): pl.pallas_call(functools.partial(kernel, chunks), out_shape=jax.ShapeDtyp...  113 us

profile of v1, /device:TPU:9, one launch (start us, length us, event | category | flops | bytes accessed | tf_op | source)
XLA Modules:
  0.0 119.8 jit_solution(1015758221144293376)
XLA Ops:
  0.0 0.7 dynamic_slice.9
  0.7 0.7 dynamic_slice.10
  1.5 0.8 select_reduce_fusion.1
  2.3 0.1 iota_compare_fusion.3
  2.4 0.7 and_select_fusion.2
  3.0 0.2 convert_reduce_fusion
  3.2 0.1 dynamic_slice.11.slot_of
  3.3 0.1 select_reduce_fusion.receive_index
  3.4 0.2 broadcast_and_fusion
  3.6 0.0 copy-start
  3.6 0.6 copy-done
  4.3 0.0 copy-start.1
  4.3 0.7 copy-done.1
  5.0 113.1 %shard_map.55 = f32[8,128,384]{2,1,0:T(8,128)S(1)} custom-call(s32[32]{0:T(128)S(1)} %select_reduce_fusion.receive_index, s32[32]{0:T(128)S(1)} %dynamic_slice.11.slot_of, s32[128]{0:T(128)S(1)} %copy-done.1, s32[128]{0:T(128)S(1)} %copy-done, bf16[32,3,128,128]{3,2,1,0:T(8,128)(2,1)} %wave_hbm.1, bf16[32,4,128,128]{3,2,1,0:T(8,128)(2,1)} %left_hbm.1, ...), custom_call_target="tpu_custom_call" | custom-call | flops 3221225472 | bytes 16777216 | tf_op jit(solution)/shard_map/pallas_call | solution.py:252
  118.1 0.5 copy.8
  118.5 1.3 %broadcast_select_fusion = f32[8,3,128,128]{3,2,1,0:T(8,128)} fusion(f32[8,3,128,128]{3,2,1,0:T(8,128)S(1)} %bitcast.3, pred[8,128,128]{2,1,0:T(8,128)(4,1)S(1)} %broadcast_and_fusion), kind=kLoop, calls=%fused_computation | loop fusion | flops 393216 | bytes 3276800 | tf_op jit(solution)/shard_map/jit(_where)/select_n | solution.py:273
  (1 shorter events, 0.0 us)
Async XLA Ops:
  3.6 0.7 copy-start
  4.3 0.7 copy-start.1

commit v2 on v1

--- a/solution.py
+++ b/solution.py
@@ -8,15 +8,14 @@
 from jax.sharding import PartitionSpec as P
 
 MESH = pl.DeviceIdType.MESH
-CHUNKS = (32, 32, 32, 16, 16)
-AHEAD = 2
-
-
-def kernel(chunks, receive_index, slot_of, sizes, partner, wave_hbm, left_hbm, right_hbm, out_ref,
-           wave, left, right, partial, *rest):
+CHUNKS = (48, 32, 32, 16)
+
+
+def kernel(chunks, receive_index, slot_of, sector_of, sizes_hbm, partner_hbm, wave_hbm, left_hbm, right_hbm, out_ref,
+           sizes, partner, wave, left, partial, products, *rest):
     n_chunks = len(chunks)
-    outgoing, arrived, sums, landed = (rest[i * n_chunks:(i + 1) * n_chunks] for i in range(4))
-    load_sem, send_sem, recv_sem, sum_send_sem, sum_recv_sem = rest[4 * n_chunks:]
+    right, outgoing, arrived, sums, landed = (rest[i * n_chunks:(i + 1) * n_chunks] for i in range(5))
+    load_sem, send_sem, recv_sem, sum_send_sem, sum_recv_sem = rest[5 * n_chunks:]
     sector_count, vecs, block, _ = wave.shape
     terms = left.shape[1]
     peers = lax.axis_size("sec")
@@ -27,12 +26,16 @@
     my_term = lax.axis_index("term")
     starts = [sum(chunks[:c]) for c in range(n_chunks)]
 
-    right_load = pltpu.make_async_copy(right_hbm, right, load_sem.at[0])
-    left_load = pltpu.make_async_copy(left_hbm, left, load_sem.at[1])
-    wave_load = pltpu.make_async_copy(wave_hbm, wave, load_sem.at[2])
-    right_load.start()
-    left_load.start()
-    wave_load.start()
+    right_loads = [
+        pltpu.make_async_copy(right_hbm.at[:, :, pl.ds(starts[c], chunks[c])], right[c], load_sem.at[4 + c])
+        for c in range(n_chunks)
+    ]
+    left_load = pltpu.make_async_copy(left_hbm, left, load_sem.at[0])
+    wave_load = pltpu.make_async_copy(wave_hbm, wave, load_sem.at[1])
+    sizes_load = pltpu.make_async_copy(sizes_hbm, sizes, load_sem.at[2])
+    partner_load = pltpu.make_async_copy(partner_hbm, partner, load_sem.at[3])
+    for load in right_loads:
+        load.start()
 
     barrier = pltpu.get_barrier_semaphore()
 
@@ -46,15 +49,13 @@
 
     lax.fori_loop(1, peers, greet_sec, 0)
     lax.fori_loop(1, owners, greet_term, 0)
-    right_load.wait()
-
     def pick(c, target, into, slot_base):
         def one(r, carry):
             index = receive_index[target * capacity + r]
             for t in range(terms):
-                into[slot_base + r, :, t * block:(t + 1) * block] = right[index, t, starts[c]:starts[c] + chunks[c], :]
-            return carry
-        lax.fori_loop(0, capacity, one, 0)
+                into[slot_base + r, :, t * block:(t + 1) * block] = right[c][index, t]
+            return carry
+        lax.fori_loop(0, capacity, one, 0, unroll=min(capacity, 4))
 
     def block_copy(c, target):
         return pltpu.make_async_remote_copy(
@@ -76,8 +77,17 @@
             device_id_type=MESH,
         )
 
+    def others(i, index, count):
+        base = index - lax.rem(index, 2)
+        far = lax.rem(base + 2 + lax.rem(i + lax.rem(index, 2), count - 2), count)
+        near = index + 1 - 2 * lax.rem(index, 2)
+        return jnp.where(i < count - 2, far, near)
+
     def far_first(i):
-        return lax.rem(me + 1 + lax.rem(i + peers // 2 - 1, peers - 1), peers)
+        return others(i, me, peers)
+
+    def owner_order(i):
+        return others(i, my_term, owners)
 
     def launch(c):
         def one(i, carry):
@@ -90,12 +100,6 @@
     def sent(c):
         def one(i, carry):
             block_copy(c, far_first(i)).wait_send()
-            return carry
-        lax.fori_loop(0, peers - 1, one, 0)
-
-    def arrive(c):
-        def one(i, carry):
-            arrival(c, far_first(i)).wait_recv()
             return carry
         lax.fori_loop(0, peers - 1, one, 0)
 
@@ -120,11 +124,19 @@
         )
 
     pl.semaphore_wait(barrier, peers - 1 + owners - 1)
-    for c in range(min(AHEAD, n_chunks)):
+    for c in range(n_chunks):
+        right_loads[c].wait()
         launch(c)
+        if c == 0:
+            sizes_load.start()
+            partner_load.start()
+            wave_load.start()
+            left_load.start()
     for c in range(n_chunks):
         pick(c, me, arrived[c], me * capacity)
 
+    sizes_load.wait()
+    partner_load.wait()
     left_load.wait()
     wave_load.wait()
     row_ids = lax.broadcasted_iota(jnp.int32, (block, block), 0)
@@ -143,12 +155,17 @@
                 partial[l, v * block:(v + 1) * block, t * block:(t + 1) * block] = product[:, v * block:(v + 1) * block]
         return carry
 
-    lax.fori_loop(0, sector_count, first_products, 0)
-
-    def second_product(c, l):
-        return lax.dot_general(
-            arrived[c][slot_of[l]], partial[l], (((1,), (1,)), ((), ())), preferred_element_type=jnp.float32
-        )
+    lax.fori_loop(0, sector_count, first_products, 0, unroll=2)
+
+    def multiply(c, source):
+        def one(r, carry):
+            slot = source * capacity + r
+            products[slot, 0:chunks[c], :] = lax.dot_general(
+                arrived[c][slot], partial[sector_of[slot]], (((1,), (1,)), ((), ())),
+                preferred_element_type=jnp.float32,
+            )
+            return carry
+        lax.fori_loop(0, capacity, one, 0, unroll=min(capacity, 4))
 
     def finish(c):
         rows = pl.ds(starts[c], chunks[c])
@@ -157,35 +174,48 @@
             sum_arrival(c, lax.rem(my_term + i, owners)).wait_recv()
             return carry
         lax.fori_loop(1, owners, wait_one, 0)
+
+        m_ids = starts[c] + lax.broadcasted_iota(jnp.int32, (chunks[c], block), 0)
+        i_ids = lax.broadcasted_iota(jnp.int32, (chunks[c], block), 1)
 
         def add(s, carry):
             total = out_ref[s, rows, :]
             for i in range(1, owners):
                 total = total + landed[c][lax.rem(my_term + i, owners), s].astype(jnp.float32)
-            out_ref[s, rows, :] = total
-            return carry
-        lax.fori_loop(0, owned, add, 0)
+            sector = me * sector_count + my_term * owned + s
+            keep = (m_ids < sizes[partner[sector]]) & (i_ids < sizes[sector])
+            for v in range(vecs):
+                out_ref[s, rows, v * block:(v + 1) * block] = jnp.where(
+                    keep, total[:, v * block:(v + 1) * block], 0.0
+                )
+            return carry
+        lax.fori_loop(0, owned, add, 0, unroll=2)
 
     for c in range(n_chunks):
-        arrive(c)
-        if c + AHEAD < n_chunks:
-            launch(c + AHEAD)
+        multiply(c, me)
+
+        def from_source(i, carry):
+            source = far_first(peers - 2 - i)
+            arrival(c, source).wait_recv()
+            multiply(c, source)
+            return carry
+        lax.fori_loop(0, peers - 1, from_source, 0)
 
         def for_owner(i, carry):
-            owner = lax.rem(my_term + i, owners)
+            owner = owner_order(i)
 
             def one(s, inner):
-                sums[c][owner, s] = second_product(c, owner * owned + s).astype(jnp.bfloat16)
+                sums[c][owner, s] = products[slot_of[owner * owned + s], 0:chunks[c], :].astype(jnp.bfloat16)
                 return inner
-            lax.fori_loop(0, owned, one, 0)
+            lax.fori_loop(0, owned, one, 0, unroll=min(owned, 4))
             sum_copy(c, owner).start()
             return carry
-        lax.fori_loop(1, owners, for_owner, 0)
+        lax.fori_loop(0, owners - 1, for_owner, 0)
 
         def for_me(s, carry):
-            out_ref[s, starts[c]:starts[c] + chunks[c], :] = second_product(c, my_term * owned + s)
-            return carry
-        lax.fori_loop(0, owned, for_me, 0)
+            out_ref[s, starts[c]:starts[c] + chunks[c], :] = products[slot_of[my_term * owned + s], 0:chunks[c], :]
+            return carry
+        lax.fori_loop(0, owned, for_me, 0, unroll=min(owned, 4))
         if c > 0:
             finish(c - 1)
     finish(n_chunks - 1)
@@ -205,7 +235,6 @@
     peers = lax.axis_size("sec")
     owners = lax.axis_size("term")
     own_index = lax.axis_index("sec")
-    term_index = lax.axis_index("term")
     capacity = sector_count // peers
     owned = sector_count // owners
     sector_ids = jnp.arange(sector_sizes.shape[0], dtype=jnp.int32)
@@ -225,23 +254,29 @@
         jnp.where(receive_key[None, :] == slot_range[:, None], (right_partner % sector_count)[None, :], 0), axis=1
     )
 
+    slot_ids = jnp.arange(sector_count, dtype=jnp.int32)
+    sector_of = jnp.sum(jnp.where(local_slot[None, :] == slot_ids[:, None], slot_ids[None, :], 0), axis=1)
+
     chunks = CHUNKS
     wide = terms * block
     columns = vecs * block
     n = len(chunks)
     vmem = lambda shape, dtype: pltpu.VMEM(shape, dtype)
     scratch = [
+        pltpu.SMEM(sector_sizes.shape, jnp.int32),
+        pltpu.SMEM(right_partner.shape, jnp.int32),
         vmem(wavefunction.shape, jnp.bfloat16),
         vmem(left_ops.shape, jnp.bfloat16),
-        vmem(right_ops.shape, jnp.bfloat16),
         vmem((sector_count, columns, wide), jnp.bfloat16),
+        vmem((sector_count, max(chunks), columns), jnp.float32),
     ]
+    scratch += [vmem((sector_count, terms, rows, block), jnp.bfloat16) for rows in chunks]
     scratch += [vmem((sector_count, rows, wide), jnp.bfloat16) for rows in chunks]
     scratch += [vmem((sector_count, rows, wide), jnp.bfloat16) for rows in chunks]
     scratch += [vmem((owners, owned, rows, columns), jnp.bfloat16) for rows in chunks]
     scratch += [vmem((owners, owned, rows, columns), jnp.bfloat16) for rows in chunks]
     scratch += [
-        pltpu.SemaphoreType.DMA((3,)),
+        pltpu.SemaphoreType.DMA((4 + n,)),
         pltpu.SemaphoreType.DMA((n, peers)),
         pltpu.SemaphoreType.DMA((n, peers)),
         pltpu.SemaphoreType.DMA((n, owners)),
@@ -252,7 +287,7 @@
     summed = pl.pallas_call(
         functools.partial(kernel, chunks),
         out_shape=jax.ShapeDtypeStruct((owned, block, columns), jnp.float32),
-        in_specs=[smem, smem, smem, smem, anywhere, anywhere, anywhere],
+        in_specs=[smem, smem, smem, anywhere, anywhere, anywhere, anywhere, anywhere],
         out_specs=pl.BlockSpec(memory_space=pltpu.VMEM),
         scratch_shapes=scratch,
         compiler_params=pltpu.CompilerParams(
@@ -261,16 +296,9 @@
         cost_estimate=pl.CostEstimate(
             flops=4 * sector_count * terms * vecs * block**3, bytes_accessed=16 * 1024 * 1024, transcendentals=0
         ),
-    )(receive_index, local_slot, sector_sizes, right_partner, wavefunction, left_ops, right_ops)
-
-    first = own_index * sector_count + term_index * owned
-    own_sizes = lax.dynamic_slice_in_dim(sector_sizes, first, owned)
-    own_partner = lax.dynamic_slice_in_dim(right_partner, first, owned)
-    right_sizes = jnp.sum(jnp.where(own_partner[:, None] == sector_ids[None, :], sector_sizes[None, :], 0), axis=1)
-    row_ids = jnp.arange(block, dtype=jnp.int32)
-    keep = (row_ids[None, :] < own_sizes[:, None])[:, :, None] & (row_ids[None, :] < right_sizes[:, None])[:, None, :]
-    sigma = summed.reshape(owned, block, vecs, block).transpose(0, 2, 3, 1)
-    return jnp.where(keep[:, None], sigma, jnp.zeros_like(sigma))
+    )(receive_index, local_slot, sector_of, sector_sizes, right_partner, wavefunction, left_ops, right_ops)
+
+    return summed.reshape(owned, block, vecs, block).transpose(0, 2, 3, 1)
 
 
 def solution(mesh):

time: 120 us -> 110 us (0.917)
  Pallas kernels: 113 us -> 106 us
  other arithmetic: 3.38 us -> 1.07 us
    pallas_call x1, Pallas kernels: 113 us -> 106 us  [on_device(): pl.pallas_call(functools.partial(kernel, chunks), out_shape=jax.ShapeDtyp...]
    dynamic_slice x2 -> x0, local copies, waits for them, and re-layouts: 1.45 us -> none  [the longest x1 0.73 us: on_device(): own_sizes = lax.dynamic_slice_in_dim(sector_sizes, first, owned)]
    select_n x1 -> x0, other arithmetic: 1.3 us -> none  [on_device(): return jnp.where(keep[:, None], sigma, jnp.zeros_like(sigma))]
where the time goes in v2:
time: 110 us
  Pallas kernels  106 us (96%)
  local copies, waits for them, and re-layouts  3.01 us (3%)
    pallas_call x1, Pallas kernels, on_device(): pl.pallas_call(functools.partial(kernel, chunks), out_shape=jax.ShapeDtyp...  106 us

profile of v2, /device:TPU:9, one launch (start us, length us, event | category | flops | bytes accessed | tf_op | source)
XLA Modules:
  0.0 110.1 jit_solution(11174631715037348267)
XLA Ops:
  0.0 0.7 and_select_fusion.2
  0.7 0.2 convert_reduce_fusion
  0.9 0.1 dynamic_slice.3.slot_of
  0.9 0.1 select_reduce_fusion.1.receive_index
  1.0 0.1 select_reduce_fusion.sector_of
  1.2 0.0 copy-start
  1.2 0.7 copy-done
  1.8 0.0 copy-start.1
  1.8 0.7 copy-done.1
  2.5 105.9 %shard_map.55 = f32[8,128,384]{2,1,0:T(8,128)S(1)} custom-call(s32[32]{0:T(128)S(1)} %select_reduce_fusion.1.receive_index, s32[32]{0:T(128)S(1)} %dynamic_slice.3.slot_of, s32[32]{0:T(128)S(1)} %select_reduce_fusion.sector_of, s32[128]{0:T(128)S(1)} %copy-done.1, s32[128]{0:T(128)S(1)} %copy-done, bf16[32,3,128,128]{3,2,1,0:T(8,128)(2,1)} %wave_hbm.1, ...), custom_call_target="tpu_custom_call" | custom-call | flops 3221225472 | bytes 16777216 | tf_op jit(solution)/shard_map/pallas_call | solution.py:287
  108.4 1.6 %copy.8 = f32[8,128,384]{1,2,0:T(8,128)} copy(f32[8,128,384]{2,1,0:T(8,128)S(1)} %shard_map.55) | data formatting | bytes 3145728 | tf_op jit(solution)/shard_map/pallas_call | solution.py:287
  (1 shorter events, 0.0 us)
Async XLA Ops:
  1.2 0.7 copy-start
  1.8 0.7 copy-start.1

commit v3 on v2

--- a/solution.py
+++ b/solution.py
@@ -86,9 +86,6 @@
     def far_first(i):
         return others(i, me, peers)
 
-    def owner_order(i):
-        return others(i, my_term, owners)
-
     def launch(c):
         def one(i, carry):
             target = far_first(i)
@@ -103,23 +100,37 @@
             return carry
         lax.fori_loop(0, peers - 1, one, 0)
 
-    def sum_copy(c, owner):
-        return pltpu.make_async_remote_copy(
-            src_ref=sums[c].at[owner],
-            dst_ref=landed[c].at[my_term],
-            send_sem=sum_send_sem.at[c, owner],
-            recv_sem=sum_recv_sem.at[c, my_term],
-            device_id={"term": owner},
-            device_id_type=MESH,
-        )
-
-    def sum_arrival(c, source):
-        return pltpu.make_async_remote_copy(
-            src_ref=sums[c].at[source],
-            dst_ref=landed[c].at[source],
-            send_sem=sum_send_sem.at[c, source],
-            recv_sem=sum_recv_sem.at[c, source],
-            device_id={"term": source},
+    half = owners // 2
+    pair = my_term // 2
+    side = lax.rem(my_term, 2)
+
+    def sibling_copy(c):
+        return pltpu.make_async_remote_copy(
+            src_ref=sums[c].at[pl.ds(0, half)],
+            dst_ref=landed[c].at[pl.ds(0, half)],
+            send_sem=sum_send_sem.at[c, 0],
+            recv_sem=sum_recv_sem.at[c, 0],
+            device_id={"term": my_term + 1 - 2 * side},
+            device_id_type=MESH,
+        )
+
+    def pair_copy(c, other):
+        return pltpu.make_async_remote_copy(
+            src_ref=sums[c].at[half + other],
+            dst_ref=landed[c].at[half + pair],
+            send_sem=sum_send_sem.at[c, 1 + other],
+            recv_sem=sum_recv_sem.at[c, 1 + pair],
+            device_id={"term": 2 * other + side},
+            device_id_type=MESH,
+        )
+
+    def pair_arrival(c, other):
+        return pltpu.make_async_remote_copy(
+            src_ref=sums[c].at[half + other],
+            dst_ref=landed[c].at[half + other],
+            send_sem=sum_send_sem.at[c, 1 + other],
+            recv_sem=sum_recv_sem.at[c, 1 + other],
+            device_id={"term": 2 * other + side},
             device_id_type=MESH,
         )
 
@@ -171,17 +182,16 @@
         rows = pl.ds(starts[c], chunks[c])
 
         def wait_one(i, carry):
-            sum_arrival(c, lax.rem(my_term + i, owners)).wait_recv()
-            return carry
-        lax.fori_loop(1, owners, wait_one, 0)
-
+            pair_arrival(c, lax.rem(pair + i, half)).wait_recv()
+            return carry
+        lax.fori_loop(1, half, wait_one, 0)
         m_ids = starts[c] + lax.broadcasted_iota(jnp.int32, (chunks[c], block), 0)
         i_ids = lax.broadcasted_iota(jnp.int32, (chunks[c], block), 1)
 
         def add(s, carry):
             total = out_ref[s, rows, :]
-            for i in range(1, owners):
-                total = total + landed[c][lax.rem(my_term + i, owners), s].astype(jnp.float32)
+            for i in range(1, half):
+                total = total + landed[c][half + lax.rem(pair + i, half), s].astype(jnp.float32)
             sector = me * sector_count + my_term * owned + s
             keep = (m_ids < sizes[partner[sector]]) & (i_ids < sizes[sector])
             for v in range(vecs):
@@ -201,32 +211,49 @@
             return carry
         lax.fori_loop(0, peers - 1, from_source, 0)
 
-        def for_owner(i, carry):
-            owner = owner_order(i)
+        def for_sibling(other, carry):
+            owner = 2 * other + 1 - side
 
             def one(s, inner):
-                sums[c][owner, s] = products[slot_of[owner * owned + s], 0:chunks[c], :].astype(jnp.bfloat16)
+                sums[c][other, s] = products[slot_of[owner * owned + s], 0:chunks[c], :].astype(jnp.bfloat16)
                 return inner
             lax.fori_loop(0, owned, one, 0, unroll=min(owned, 4))
-            sum_copy(c, owner).start()
-            return carry
-        lax.fori_loop(0, owners - 1, for_owner, 0)
-
-        def for_me(s, carry):
-            out_ref[s, starts[c]:starts[c] + chunks[c], :] = products[slot_of[my_term * owned + s], 0:chunks[c], :]
-            return carry
-        lax.fori_loop(0, owned, for_me, 0, unroll=min(owned, 4))
+            return carry
+        lax.fori_loop(0, half, for_sibling, 0)
+        sibling_copy(c).start()
         if c > 0:
             finish(c - 1)
+        sibling_copy(c).wait_recv()
+
+        def for_pair(i, carry):
+            other = lax.rem(pair + i, half)
+            owner = 2 * other + side
+
+            def one(s, inner):
+                own = products[slot_of[owner * owned + s], 0:chunks[c], :]
+                sums[c][half + other, s] = (own + landed[c][other, s].astype(jnp.float32)).astype(jnp.bfloat16)
+                return inner
+            lax.fori_loop(0, owned, one, 0, unroll=min(owned, 4))
+            pair_copy(c, other).start()
+            return carry
+        lax.fori_loop(1, half, for_pair, 0)
+
+        def for_me(s, carry):
+            own = products[slot_of[my_term * owned + s], 0:chunks[c], :]
+            out_ref[s, starts[c]:starts[c] + chunks[c], :] = own + landed[c][pair, s].astype(jnp.float32)
+            return carry
+        lax.fori_loop(0, owned, for_me, 0, unroll=min(owned, 4))
     finish(n_chunks - 1)
 
     for c in range(n_chunks):
         sent(c)
 
+        sibling_copy(c).wait_send()
+
         def sum_sent(i, carry):
-            sum_copy(c, lax.rem(my_term + i, owners)).wait_send()
-            return carry
-        lax.fori_loop(1, owners, sum_sent, 0)
+            pair_copy(c, lax.rem(pair + i, half)).wait_send()
+            return carry
+        lax.fori_loop(1, half, sum_sent, 0)
 
 
 def on_device(wavefunction, left_ops, right_ops, sector_sizes, right_partner):

time: 110 us -> 108 us (0.982); the launches traced: 110 us -> 107 us
  Pallas kernels: 106 us -> 103 us
    pallas_call x1, Pallas kernels: 106 us -> 103 us  [on_device(): pl.pallas_call(functools.partial(kernel, chunks), out_shape=jax.ShapeDtyp...]
where the time goes in v3:
time: 108 us; the launch traced here: 107 us
  Pallas kernels  103 us (95%)
  local copies, waits for them, and re-layouts  3.01 us (3%)
    pallas_call x1, Pallas kernels, on_device(): pl.pallas_call(functools.partial(kernel, chunks), out_shape=jax.ShapeDtyp...  103 us

profile of v3, /device:TPU:9, one launch (start us, length us, event | category | flops | bytes accessed | tf_op | source)
XLA Modules:
  0.0 106.9 jit_solution(7749928552067755975)
XLA Ops:
  0.0 0.7 and_select_fusion.2
  0.7 0.2 convert_reduce_fusion
  0.9 0.1 dynamic_slice.3.slot_of
  0.9 0.1 select_reduce_fusion.1.receive_index
  1.0 0.1 select_reduce_fusion.sector_of
  1.2 0.0 copy-start
  1.2 0.7 copy-done
  1.8 0.0 copy-start.1
  1.8 0.7 copy-done.1
  2.5 102.8 %shard_map.55 = f32[8,128,384]{2,1,0:T(8,128)S(1)} custom-call(s32[32]{0:T(128)S(1)} %select_reduce_fusion.1.receive_index, s32[32]{0:T(128)S(1)} %dynamic_slice.3.slot_of, s32[32]{0:T(128)S(1)} %select_reduce_fusion.sector_of, s32[128]{0:T(128)S(1)} %copy-done.1, s32[128]{0:T(128)S(1)} %copy-done, bf16[32,3,128,128]{3,2,1,0:T(8,128)(2,1)} %wave_hbm.1, ...), custom_call_target="tpu_custom_call" | custom-call | flops 3221225472 | bytes 16777216 | tf_op jit(solution)/shard_map/pallas_call | solution.py:314
  105.3 1.6 %copy.8 = f32[8,128,384]{1,2,0:T(8,128)} copy(f32[8,128,384]{2,1,0:T(8,128)S(1)} %shard_map.55) | data formatting | bytes 3145728 | tf_op jit(solution)/shard_map/pallas_call | solution.py:314
  (1 shorter events, 0.0 us)
Async XLA Ops:
  1.2 0.7 copy-start
  1.8 0.7 copy-start.1
